TPU v7x, 32 devices: a whole 2x2x4 slice. The times are simulated.
32 devices in a mesh: pos: 8 (over y, x, core), vel: 4 (over z).
Axes of the slice: x: 2, y: 2, z: 4, core: 2. Of those that a mesh axis runs over, the one named last changes fastest.
Arguments:
- density: float32 [4, 512, 512], P(None, 'pos', 'vel'), may hold values from 0.25 to 4
- pos_coef: float32 [512, 512], P('pos', 'vel'), may hold values from 2000 to 16000
- vel_coef: float32 [512, 512], P('pos', 'vel'), may hold values from 4000 to 32000
- exit_mask: int32 [512, 512], P('pos', 'vel'), may hold values from 0 to 1, as said below
- phase_index: int32 [4], replicated, may hold values from 0 to 63
Outputs:
- new_density: float32 [4, 512, 512], P(None, 'pos', 'vel')
- absorbed: float32 [512, 512], P('pos', 'vel')
Inputs may be any that keep to these rules, and one draw needn't show every extreme that they name: exit_mask is 1 on every cell whose xpos lies beyond 1.3 in magnitude, and on scattered cells elsewhere.
All inputs are finite; a program needn't handle non-finite values.
Results may differ from a plain program's by a relative error of at most 0.0003.
Values sent between devices are 32-bit elements; how exact they have to be, the bound alone decides.
A program may use at most 64 MiB of HBM per device.

v0:
```python
import math

import jax
import jax.numpy as jnp
from jax import lax
from jax.sharding import PartitionSpec as P

STEPS = 2
NPHASE = 64


def extended(cells, sides, width):
    for axis, dim in sides:
        count = lax.axis_size(axis)
        ends = count - 1
        head = lax.slice_in_dim(cells, 0, width, axis=dim)
        tail = lax.slice_in_dim(cells, cells.shape[dim] - width, cells.shape[dim], axis=dim)
        cells = jnp.concatenate(
            [
                lax.ppermute(tail, axis, [(i, (i + 1) % count) for i in range(ends)]),
                cells,
                lax.ppermute(head, axis, [((i + 1) % count, i) for i in range(ends)]),
            ],
            axis=dim,
        )
    return cells


def thomas(below, middle, above, source):
    zero = jnp.zeros_like(source[0])

    def thomas_downward(carry, row):
        prior_up, prior_src = carry
        row_low, row_mid, row_up, row_src = row
        factor = 1.0 / (row_mid - row_low * prior_up)
        result = (factor * row_up, factor * (row_src - row_low * prior_src))
        return (result, result)

    _, (sweep_up, sweep_src) = lax.scan(
        thomas_downward, (zero, zero), (below, middle, above, source)
    )

    def thomas_upward(later, row):
        row_up, row_src = row
        value = row_src - row_up * later
        return (value, value)

    _, solved = lax.scan(thomas_upward, zero, (sweep_up, sweep_src), reverse=True)
    return solved


def drift(padded, move_rate, force_rate):
    center = padded[:, 1:-1, 1:-1]
    back_x = padded[:, :-2, 1:-1]
    ahead_x = padded[:, 2:, 1:-1]
    back_v = padded[:, 1:-1, :-2]
    ahead_v = padded[:, 1:-1, 2:]
    along_x = jnp.maximum(move_rate, 0.0) * (center - back_x) + jnp.minimum(move_rate, 0.0) * (
        ahead_x - center
    )
    along_v = jnp.maximum(force_rate, 0.0) * (center - back_v) + jnp.minimum(force_rate, 0.0) * (
        ahead_v - center
    )
    return center - along_x - along_v


def coef_factor(below, middle, above):
    inv_first = 1.0 / middle[0]
    first_low = below[0] * inv_first
    first_up = above[0] * inv_first
    inv_second = 1.0 / middle[1]
    second_low = below[1] * inv_second
    second_up = above[1] * inv_second

    def coef_downward(carry, row):
        prior_low, prior_up = carry
        row_low, row_mid, row_up = row
        factor = 1.0 / (row_mid - row_low * prior_up)
        result = (-factor * row_low * prior_low, factor * row_up)
        return (result, (result[0], result[1], factor))

    _, (rest_low, rest_up, rest_factor) = lax.scan(
        coef_downward, (second_low, second_up), (below[2:], middle[2:], above[2:])
    )
    fwd_low = jnp.concatenate([second_low[None], rest_low], axis=0)
    fwd_up = jnp.concatenate([second_up[None], rest_up], axis=0)
    fwd_factor = jnp.concatenate([inv_second[None], rest_factor], axis=0)

    def coef_upward(carry, row):
        later_low, later_up = carry
        row_low, row_up = row
        result = (row_low - row_up * later_low, -row_up * later_up)
        return (result, result)

    zero = jnp.zeros_like(first_low)
    _, (in_low, in_up) = lax.scan(
        coef_upward, (zero, -jnp.ones_like(zero)), (fwd_low[:-1], fwd_up[:-1]), reverse=True
    )
    top_factor = 1.0 / (1.0 - first_up * in_low[0])
    ends_low = jnp.stack([top_factor * first_low, fwd_low[-1]])
    ends_up = jnp.stack([-top_factor * first_up * in_up[0], fwd_up[-1]])
    return (
        inv_first,
        first_up,
        top_factor,
        fwd_factor,
        below,
        fwd_up,
        in_low,
        in_up,
        ends_low,
        ends_up,
    )


def eliminate(coefs, source):
    inv_first, first_up, top_factor, fwd_factor, below, fwd_up, in_low, in_up, ends_low, ends_up = (
        coefs
    )
    start = fwd_factor[0] * source[1]

    def eliminate_downward(prior, row):
        factor, row_low, row_src = row
        value = factor * (row_src - row_low * prior)
        return (value, value)

    _, rest = lax.scan(eliminate_downward, start, (fwd_factor[1:], below[2:], source[2:]))
    fwd_src = jnp.concatenate([start[None], rest], axis=0)

    def eliminate_upward(later, row):
        row_up, row_src = row
        value = row_src - row_up * later
        return (value, value)

    _, in_src = lax.scan(
        eliminate_upward, jnp.zeros_like(start), (fwd_up[:-1], fwd_src[:-1]), reverse=True
    )
    top_src = top_factor * (inv_first * source[0] - first_up * in_src[0])
    reduced = (ends_low, ends_up, jnp.stack([top_src, fwd_src[-1]]))
    return (reduced, (in_low, in_up, in_src))


def finish(ends, inner):
    middle_rows = inner[2] - inner[0] * ends[0] - inner[1] * ends[1]
    return jnp.concatenate([ends[0][None], middle_rows, ends[1][None]], axis=0)


def line_bands(coef, index, count):
    length = coef.shape[0]
    rows = jnp.arange(length)[:, None]
    below = jnp.where((rows == 0) & (index == 0), 0.0, -coef)
    above = jnp.where((rows == length - 1) & (index == count - 1), 0.0, -coef)
    return (below, 1.0 + 2.0 * coef, above)


def prepare_pos(pos_coef, planes):
    cells, width = pos_coef.shape
    wide = jnp.broadcast_to(pos_coef[:, None, :], (cells, planes, width)).reshape(cells, -1)
    return coef_factor(*line_bands(wide, lax.axis_index("pos"), lax.axis_size("pos")))


def prepare_vel(vel_coef, planes):
    cells, width = vel_coef.shape
    wide = jnp.broadcast_to(vel_coef.T[:, None, :], (width, planes, cells)).reshape(width, -1)
    return coef_factor(*line_bands(wide, lax.axis_index("vel"), lax.axis_size("vel")))


def along_pos(field, factored):
    index = lax.axis_index("pos")
    planes, cells, width = field.shape
    source = jnp.moveaxis(field, 1, 0).reshape(cells, planes * width)
    (low_rows, high_rows, src_rows), inner = eliminate(factored, source)
    whole_low, whole_high, whole_src = (
        lax.all_gather(low_rows, "pos", axis=0, tiled=True),
        lax.all_gather(high_rows, "pos", axis=0, tiled=True),
        lax.all_gather(src_rows, "pos", axis=0, tiled=True),
    )
    solved = thomas(whole_low, jnp.ones_like(whole_src), whole_high, whole_src)
    ends = lax.dynamic_slice_in_dim(solved, 2 * index, 2, 0)
    result = finish(ends, inner)
    return jnp.moveaxis(result.reshape(cells, planes, width), 0, 1)


def along_vel(field, factored):
    index = lax.axis_index("vel")
    planes, cells, width = field.shape
    source = jnp.moveaxis(field, 2, 0).reshape(width, planes * cells)
    (low_rows, high_rows, src_rows), inner = eliminate(factored, source)
    whole_low, whole_high, whole_src = (
        lax.all_gather(low_rows, "vel", axis=0, tiled=True),
        lax.all_gather(high_rows, "vel", axis=0, tiled=True),
        lax.all_gather(src_rows, "vel", axis=0, tiled=True),
    )
    solved = thomas(whole_low, jnp.ones_like(whole_src), whole_high, whole_src)
    ends = lax.dynamic_slice_in_dim(solved, 2 * index, 2, 0)
    result = finish(ends, inner)
    return jnp.moveaxis(result.reshape(width, planes, cells), 0, 2)


def on_device(density, pos_coef, vel_coef, exit_mask, phase_index):
    cells, width = pos_coef.shape
    planes = density.shape[0]
    pos_count = lax.axis_size("pos")
    vel_count = lax.axis_size("vel")
    pos_first = lax.axis_index("pos") * cells
    vel_first = lax.axis_index("vel") * width
    xpos = 1.5 * (
        (2.0 * (pos_first + jnp.arange(cells)).astype(jnp.float32) + 1.0) / (cells * pos_count)
        - 1.0
    )
    vpos = (2.0 * (vel_first + jnp.arange(width)).astype(jnp.float32) + 1.0) / (
        width * vel_count
    ) - 1.0
    theta = 2.0 * math.pi * phase_index.astype(jnp.float32) / NPHASE
    force = (
        (xpos - xpos * xpos * xpos)[None, :, None]
        + 0.6 * jnp.cos(theta)[:, None, None]
        - 0.5 * vpos[None, None, :]
    )
    move_rate = 0.45 * vpos[None, None, :]
    force_rate = 0.15 * force
    hit = exit_mask.astype(jnp.float32)
    keep = 1.0 - hit
    pos_factored = prepare_pos(pos_coef, planes)
    vel_factored = prepare_vel(vel_coef, planes)
    field = density
    absorbed = jnp.zeros((cells, width), jnp.float32)
    for step in range(STEPS):
        padded = extended(field, (("pos", 1), ("vel", 2)), 1)
        drifted = drift(padded, move_rate, force_rate)
        absorbed = absorbed + jnp.sum(drifted, axis=0) * hit
        kept = drifted * keep[None]
        swept = along_pos(kept, pos_factored)
        solved = along_vel(swept, vel_factored)
        field = solved * keep[None]
    return (field, absorbed)


def solution(mesh):
    return jax.shard_map(
        on_device,
        mesh=mesh,
        in_specs=(P(None, "pos", "vel"), P("pos", "vel"), P("pos", "vel"), P("pos", "vel"), P()),
        out_specs=(P(None, "pos", "vel"), P("pos", "vel")),
        check_vma=False,
    )
```

profile of v0, /device:TPU:0, one launch (start us, length us, event | category | flops | bytes accessed | tf_op | source)
XLA Modules:
  0.0 308.7 jit_solution(12233861629180539736)
XLA Ops:
  0.6 0.7 fusion.79
  1.4 1.3 collective-permute-start.1
  2.7 3.0 collective-permute-start
  6.0 0.5 copy-done.4
  6.6 0.8 copy-done.3
  8.3 0.9 copy-done
  9.3 1.3 collective-permute-start.3
  10.6 5.6 %collective-permute-start.2 = (f32[4,66,1]{2,1,0:T(8,128)S(1)}, f32[4,66,1]{2,1,0:T(8,128)S(1)}, u32[]{:S(2)}, u32[]{:S(2)}) collective-permute-start(f32[4,66,1]{2,1,0:T(8,128)S(1)} %get-tuple-element.2269), channel_id=1, source_target_pairs={{0,1},{1,2},{2,3},{4,5},{5,6},{6,7},{8,9},{9,10},{10,11},{12,13},{... | collective-permute-start | bytes 3176 | tf_op jit(solution)/shard_map/ppermute | solution.py:20
  16.4 2.0 collective-permute-done.3
  18.4 1.7 collective-permute-done.2
  20.0 0.2 fusion.72
  20.4 18.4 %while.331 = (s32[]{:T(128)}, f32[512]{0:T(512)S(1)}, f32[512]{0:T(512)S(1)}, f32[62,512]{1,0:T(8,128)S(1)}, f32[62,512]{1,0:T(8,128)S(1)}, /*index=5*/f32[62,51...) while((s32[]{:T(128)}, f32[512]{0:T(512)S(1)}, ...), condition=%wide.region_5.6_spmd, body=%wide.region_4.5_spmd.sunk | while | flops 3586 | bytes 45193 | solution.py:82
  38.9 12.3 %while.337 = (s32[]{:T(128)}, f32[512]{0:T(512)S(1)}, f32[512]{0:T(512)S(1)}, f32[62,512]{1,0:T(8,128)S(1)}, f32[62,512]{1,0:T(8,128)S(1)}, /*index=5*/f32[62,51...) while((s32[]{:T(128)}, f32[512]{0:T(512)S(1)}, f32[512]{0:T(512)S(1)}, ...), condition=%wide.region_7.8_spmd.clone, body=%wide.region_6.7_spmd.clone.sunk | while | flops 3076 | bytes 28815 | solution.py:96
  51.4 8.7 %while.332 = (s32[]{:T(128)}, f32[512]{0:T(512)S(1)}, f32[62,512]{1,0:T(8,128)S(1)}, f32[62,512]{1,0:T(8,128)S(1)}, f32[62,512]{1,0:T(8,128)S(1)}, /*index=5*/f32[62,512]{1,0:T(8,128)S(1)}, s32[]{:T(128)}, s32[]{:T(128)}) while((s32[]{:T(128)}, f32[512]{0:T(512)S(1)}, f32[62,512]{1,0:T(8,128)S(1)}, f32[62,512]{1,0:T(8,128)S(1)}, ...), condition=%wide.region_9.10_spmd, body=%wide.region_8.9_spmd.sunk | while | flops 1538 | bytes 26729 | solution.py:127
  60.2 7.9 %while.338 = (s32[]{:T(128)}, f32[512]{0:T(512)S(1)}, f32[62,512]{1,0:T(8,128)S(1)}, f32[62,512]{1,0:T(8,128)S(1)}, f32[62,512]{1,0:T(8,128)S(1)}, /*index=5*/s32[]{:T(128)}, s32[]{:T(128)}, s32[]{:T(128)}) while((s32[]{:T(128)}, f32[512]{0:T(512)S(1)}, f32[62,512]{1,0:T(8,128)S(1)}, f32[62,512]{1,0:T(8,128)S(1)}, ...), condition=%wide.region_11.12_spmd.clone, body=%wide.region_10.11_spmd.clone.sunk | while | flops 1540 | bytes 20603 | solution.py:135
  68.2 9.7 %all-gather.2 = f32[8,2,512]{2,1,0:T(2,128)S(1)} all-gather(f32[1,2,512]{2,1,0:T(2,128)S(1)} %maximum_bitcast_fusion), channel_id=1, replica_groups=mesh['pos'=8,'vel'=4] {'pos'}, dimensions={0}, use_global_device_ids=true | all-gather | bytes 36864 | tf_op jit(solution)/shard_map/all_gather | solution.py:174
  77.9 7.9 %all-gather.3 = f32[8,2,512]{2,1,0:T(2,128)S(1)} all-gather(f32[1,2,512]{2,1,0:T(2,128)S(1)} %maximum_bitcast_fusion.1), channel_id=1, replica_groups=mesh['pos'=8,'vel'=4] {'pos'}, dimensions={0}, use_global_device_ids=true | all-gather | bytes 36864 | tf_op jit(solution)/shard_map/all_gather | solution.py:175
  85.8 9.3 %all-gather.4 = f32[8,2,512]{2,1,0:T(2,128)S(1)} all-gather(f32[1,2,512]{2,1,0:T(2,128)S(1)} %maximum_bitcast_fusion.2), channel_id=1, replica_groups=mesh['pos'=8,'vel'=4] {'pos'}, dimensions={0}, use_global_device_ids=true | all-gather | bytes 36864 | tf_op jit(solution)/shard_map/all_gather | solution.py:176
  95.1 3.5 %while.339 = (s32[]{:T(128)}, f32[512]{0:T(512)S(1)}, f32[512]{0:T(512)S(1)}, f32[16,512]{1,0:T(8,128)S(1)}, f32[16,512]{1,0:T(8,128)S(1)}, /*index=5*/f32[16,51...) while((s32[]{:T(128)}, f32[512]{0:T(512)S(1)}, ...), condition=%wide.region_13.14_spmd.clone, body=%wide.region_12.13_spmd.clone.sunk | while | flops 4611 | bytes 34951 | solution.py:39
  98.7 2.0 while.340
  101.5 28.8 %while.330 = (s32[]{:T(128)}, f32[256]{0:T(256)S(1)}, f32[256]{0:T(256)S(1)}, f32[126,256]{1,0:T(8,128)S(1)}, f32[126,256]{1,0:T(8,128)S(1)}, /*index=5*/f32[126...) while((s32[]{:T(128)}, f32[256]{0:T(256)S(1)}, ...), condition=%wide.region_1.2_spmd, body=%wide.region_0.1_spmd.sunk | while | flops 1794 | bytes 22665 | solution.py:82
  130.4 19.4 %while.336 = (s32[]{:T(128)}, f32[256]{0:T(256)S(1)}, f32[256]{0:T(256)S(1)}, f32[126,256]{1,0:T(8,128)S(1)}, f32[126,256]{1,0:T(8,128)S(1)}, /*index=5*/f32[126...) while((s32[]{:T(128)}, f32[256]{0:T(256)S(1)}, f32[256]{0:T(256)S(1)}, ...), condition=%wide.region_3.4_spmd.clone, body=%wide.region_2.3_spmd.clone.sunk | while | flops 1540 | bytes 14479 | solution.py:96
  149.9 14.7 %while.333 = (s32[]{:T(128)}, f32[256]{0:T(256)S(1)}, f32[126,256]{1,0:T(8,128)S(1)}, f32[126,256]{1,0:T(8,128)S(1)}, f32[126,256]{1,0:T(8,128)S(1)}, /*index=5*/f32[126,256]{1,0:T(8,128)S(1)}, s32[]{:T(128)}, s32[]{:T(128)}) while((s32[]{:T(128)}, f32[256]{0:T(256)S(1)}, f32[126,256]{1,0:T(8,128)S(1)}, f32[126,256]{1,0:T(8,128)S(1)}, ...), condition=%wide.region_17.18_spmd, body=%wide.region_16.17_spmd.sunk | while | flops 770 | bytes 13417 | solution.py:127
  164.6 13.1 %while.341 = (s32[]{:T(128)}, f32[256]{0:T(256)S(1)}, f32[126,256]{1,0:T(8,128)S(1)}, f32[126,256]{1,0:T(8,128)S(1)}, f32[126,256]{1,0:T(8,128)S(1)}, /*index=5*/s32[]{:T(128)}, s32[]{:T(128)}, s32[]{:T(128)}) while((s32[]{:T(128)}, f32[256]{0:T(256)S(1)}, f32[126,256]{1,0:T(8,128)S(1)}, f32[126,256]{1,0:T(8,128)S(1)}, ...), condition=%wide.region_19.20_spmd.clone, body=%wide.region_18.19_spmd.clone.sunk | while | flops 772 | bytes 10363 | solution.py:135
  177.9 13.0 %all-gather = f32[4,2,256]{2,1,0:T(2,128)S(1)} all-gather(f32[1,2,256]{2,1,0:T(2,128)S(1)} %maximum_bitcast_fusion.4), channel_id=1, replica_groups=mesh['pos'=8,'vel'=4] {'vel'}, dimensions={0}, use_global_device_ids=true | all-gather | bytes 10240 | tf_op jit(solution)/shard_map/all_gather | solution.py:190
  191.0 11.9 %all-gather.1 = f32[4,2,256]{2,1,0:T(2,128)S(1)} all-gather(f32[1,2,256]{2,1,0:T(2,128)S(1)} %maximum_bitcast_fusion.5), channel_id=1, replica_groups=mesh['pos'=8,'vel'=4] {'vel'}, dimensions={0}, use_global_device_ids=true | all-gather | bytes 10240 | tf_op jit(solution)/shard_map/all_gather | solution.py:191
  202.8 11.9 %all-gather.5 = f32[4,2,256]{2,1,0:T(2,128)S(1)} all-gather(f32[1,2,256]{2,1,0:T(2,128)S(1)} %maximum_bitcast_fusion.6), channel_id=1, replica_groups=mesh['pos'=8,'vel'=4] {'vel'}, dimensions={0}, use_global_device_ids=true | all-gather | bytes 10240 | tf_op jit(solution)/shard_map/all_gather | solution.py:192
  214.8 1.3 while.342
  216.1 0.8 while.343
  217.1 1.3 collective-permute-start.5
  218.4 3.0 collective-permute-start.4
  221.5 0.8 collective-permute-done.4
  222.4 1.3 collective-permute-start.7
  223.7 4.6 %collective-permute-start.6 = (f32[4,66,1]{2,1,0:T(8,128)S(1)}, f32[4,66,1]{2,1,0:T(8,128)S(1)}, u32[]{:S(2)}, u32[]{:S(2)}) collective-permute-start(f32[4,66,1]{2,1,0:T(8,128)S(1)} %get-tuple-element.2267), channel_id=1, source_target_pairs={{0,1},{1,2},{2,3},{4,5},{5,6},{6,7},{8,9},{9,10},{10,11},{12,13},{... | collective-permute-start | bytes 3176 | tf_op jit(solution)/shard_map/ppermute | solution.py:20
  228.3 2.0 collective-permute-done.7
  230.4 1.2 collective-permute-done.6
  232.0 8.7 %while.334 = (s32[]{:T(128)}, f32[512]{0:T(512)S(1)}, f32[62,512]{1,0:T(8,128)S(1)}, f32[62,512]{1,0:T(8,128)S(1)}, f32[62,512]{1,0:T(8,128)S(1)}, /*index=5*/f32[62,512]{1,0:T(8,128)S(1)}, s32[]{:T(128)}, s32[]{:T(128)}) while((s32[]{:T(128)}, f32[512]{0:T(512)S(1)}, f32[62,512]{1,0:T(8,128)S(1)}, f32[62,512]{1,0:T(8,128)S(1)}, ...), condition=%wide.region_25.26_spmd, body=%wide.region_24.25_spmd.sunk | while | flops 1538 | bytes 26729 | solution.py:127
  240.8 7.9 %while.344 = (s32[]{:T(128)}, f32[512]{0:T(512)S(1)}, f32[62,512]{1,0:T(8,128)S(1)}, f32[62,512]{1,0:T(8,128)S(1)}, f32[62,512]{1,0:T(8,128)S(1)}, /*index=5*/s32[]{:T(128)}, s32[]{:T(128)}, s32[]{:T(128)}) while((s32[]{:T(128)}, f32[512]{0:T(512)S(1)}, f32[62,512]{1,0:T(8,128)S(1)}, f32[62,512]{1,0:T(8,128)S(1)}, ...), condition=%wide.region_27.28_spmd.clone, body=%wide.region_26.27_spmd.clone.sunk | while | flops 1540 | bytes 20603 | solution.py:135
  248.7 10.0 %all-gather.6 = f32[8,2,512]{2,1,0:T(2,128)S(1)} all-gather(f32[1,2,512]{2,1,0:T(2,128)S(1)} %maximum_bitcast_fusion.3), channel_id=1, replica_groups=mesh['pos'=8,'vel'=4] {'pos'}, dimensions={0}, use_global_device_ids=true | all-gather | bytes 36864 | tf_op jit(solution)/shard_map/all_gather | solution.py:176
  258.7 3.5 %while.345 = (s32[]{:T(128)}, f32[512]{0:T(512)S(1)}, f32[512]{0:T(512)S(1)}, f32[16,512]{1,0:T(8,128)S(1)}, f32[16,512]{1,0:T(8,128)S(1)}, /*index=5*/f32[16,51...) while((s32[]{:T(128)}, f32[512]{0:T(512)S(1)}, ...), condition=%wide.region_29.30_spmd.clone, body=%wide.region_28.29_spmd.clone.sunk | while | flops 4611 | bytes 34951 | solution.py:39
  262.3 2.0 while.346
  265.2 14.7 %while.335 = (s32[]{:T(128)}, f32[256]{0:T(256)S(1)}, f32[126,256]{1,0:T(8,128)S(1)}, f32[126,256]{1,0:T(8,128)S(1)}, f32[126,256]{1,0:T(8,128)S(1)}, /*index=5*/f32[126,256]{1,0:T(8,128)S(1)}, s32[]{:T(128)}, s32[]{:T(128)}) while((s32[]{:T(128)}, f32[256]{0:T(256)S(1)}, f32[126,256]{1,0:T(8,128)S(1)}, f32[126,256]{1,0:T(8,128)S(1)}, ...), condition=%wide.region_33.34_spmd, body=%wide.region_32.33_spmd.sunk | while | flops 770 | bytes 13417 | solution.py:127
  279.9 13.1 %while.347 = (s32[]{:T(128)}, f32[256]{0:T(256)S(1)}, f32[126,256]{1,0:T(8,128)S(1)}, f32[126,256]{1,0:T(8,128)S(1)}, f32[126,256]{1,0:T(8,128)S(1)}, /*index=5*/s32[]{:T(128)}, s32[]{:T(128)}, s32[]{:T(128)}) while((s32[]{:T(128)}, f32[256]{0:T(256)S(1)}, f32[126,256]{1,0:T(8,128)S(1)}, f32[126,256]{1,0:T(8,128)S(1)}, ...), condition=%wide.region_35.36_spmd.clone, body=%wide.region_34.35_spmd.clone.sunk | while | flops 772 | bytes 10363 | solution.py:135
  293.2 11.9 %all-gather.7 = f32[4,2,256]{2,1,0:T(2,128)S(1)} all-gather(f32[1,2,256]{2,1,0:T(2,128)S(1)} %maximum_bitcast_fusion.7), channel_id=1, replica_groups=mesh['pos'=8,'vel'=4] {'vel'}, dimensions={0}, use_global_device_ids=true | all-gather | bytes 10240 | tf_op jit(solution)/shard_map/all_gather | solution.py:192
  305.1 1.3 while.348
  306.4 0.8 while.349
  307.4 0.7 broadcast_multiply_fusion
  308.1 0.6 add_multiply_fusion
  (5278 shorter events, 137.1 us)
Async XLA Ops:
  0.6 5.1 %copy-start.2 = (f32[64,128]{1,0:T(8,128)S(1)}, f32[64,128]{1,0:T(8,128)}, u32[]{:S(2)}) copy-start(f32[64,128]{1,0:T(8,128)} %param.47) | copy-start | bytes 98308
  1.4 6.9 %collective-permute-start.1 = (f32[4,1,128]{2,1,0:T(1,128)S(1)}, f32[4,1,128]{2,1,0:T(1,128)S(1)}, u32[]{:S(2)}, u32[]{:S(2)}) collective-permute-start(f32[4,1,128]{2,1,0:T(1,128)S(1)} %get-tuple-element.2286), channel_id=1, source_target_pairs={{4,0},{8,4},{12,8},{16,12},{20,16},{24,20},{28,24},{5,1},{9,5},{13... | collective-permute-start | bytes 6152 | tf_op jit(solution)/shard_map/ppermute | solution.py:22
  2.7 5.6 %collective-permute-start = (f32[4,1,128]{2,1,0:T(1,128)S(1)}, f32[4,1,128]{2,1,0:T(1,128)S(1)}, u32[]{:S(2)}, u32[]{:S(2)}) collective-permute-start(f32[4,1,128]{2,1,0:T(1,128)S(1)} %get-tuple-element.2285), channel_id=1, source_target_pairs={{0,4},{4,8},{8,12},{12,16},{16,20},{20,24},{24,28},{1,5},{5,9},{9,... | collective-permute-start | bytes 6152 | tf_op jit(solution)/shard_map/ppermute | solution.py:20
  5.8 0.7 copy-start.4
  5.8 0.8 copy-start.1
  6.6 0.8 copy-start.3
  8.2 0.9 copy-start
  9.3 9.1 %collective-permute-start.3 = (f32[4,66,1]{2,1,0:T(8,128)S(1)}, f32[4,66,1]{2,1,0:T(8,128)S(1)}, u32[]{:S(2)}, u32[]{:S(2)}) collective-permute-start(f32[4,66,1]{2,1,0:T(8,128)S(1)} %get-tuple-element.2270), channel_id=1, source_target_pairs={{1,0},{2,1},{3,2},{5,4},{6,5},{7,6},{9,8},{10,9},{11,10},{13,12},{... | collective-permute-start | bytes 3176 | tf_op jit(solution)/shard_map/ppermute | solution.py:22
  10.6 9.5 %collective-permute-start.2 = (f32[4,66,1]{2,1,0:T(8,128)S(1)}, f32[4,66,1]{2,1,0:T(8,128)S(1)}, u32[]{:S(2)}, u32[]{:S(2)}) collective-permute-start(f32[4,66,1]{2,1,0:T(8,128)S(1)} %get-tuple-element.2269), channel_id=1, source_target_pairs={{0,1},{1,2},{2,3},{4,5},{5,6},{6,7},{8,9},{9,10},{10,11},{12,13},{... | collective-permute-start | bytes 3176 | tf_op jit(solution)/shard_map/ppermute | solution.py:20
  217.1 4.3 %collective-permute-start.5 = (f32[4,1,128]{2,1,0:T(1,128)S(1)}, f32[4,1,128]{2,1,0:T(1,128)S(1)}, u32[]{:S(2)}, u32[]{:S(2)}) collective-permute-start(f32[4,1,128]{2,1,0:T(1,128)S(1)} %get-tuple-element.2274), channel_id=1, source_target_pairs={{4,0},{8,4},{12,8},{16,12},{20,16},{24,20},{28,24},{5,1},{9,5},{13... | collective-permute-start | bytes 6152 | tf_op jit(solution)/shard_map/ppermute | solution.py:22
  218.4 3.8 %collective-permute-start.4 = (f32[4,1,128]{2,1,0:T(1,128)S(1)}, f32[4,1,128]{2,1,0:T(1,128)S(1)}, u32[]{:S(2)}, u32[]{:S(2)}) collective-permute-start(f32[4,1,128]{2,1,0:T(1,128)S(1)} %get-tuple-element.2273), channel_id=1, source_target_pairs={{0,4},{4,8},{8,12},{12,16},{16,20},{20,24},{24,28},{1,5},{5,9},{9,... | collective-permute-start | bytes 6152 | tf_op jit(solution)/shard_map/ppermute | solution.py:20
  222.4 8.0 %collective-permute-start.7 = (f32[4,66,1]{2,1,0:T(8,128)S(1)}, f32[4,66,1]{2,1,0:T(8,128)S(1)}, u32[]{:S(2)}, u32[]{:S(2)}) collective-permute-start(f32[4,66,1]{2,1,0:T(8,128)S(1)} %get-tuple-element.2268), channel_id=1, source_target_pairs={{1,0},{2,1},{3,2},{5,4},{6,5},{7,6},{9,8},{10,9},{11,10},{13,12},{... | collective-permute-start | bytes 3176 | tf_op jit(solution)/shard_map/ppermute | solution.py:22
  223.7 7.9 %collective-permute-start.6 = (f32[4,66,1]{2,1,0:T(8,128)S(1)}, f32[4,66,1]{2,1,0:T(8,128)S(1)}, u32[]{:S(2)}, u32[]{:S(2)}) collective-permute-start(f32[4,66,1]{2,1,0:T(8,128)S(1)} %get-tuple-element.2267), channel_id=1, source_target_pairs={{0,1},{1,2},{2,3},{4,5},{5,6},{6,7},{8,9},{9,10},{10,11},{12,13},{... | collective-permute-start | bytes 3176 | tf_op jit(solution)/shard_map/ppermute | solution.py:20
where the time goes:
time: 309 us
  local copies, waits for them, and re-layouts  119 us (39%)
  blocking collectives  85.5 us (28%)
  loops' own time  50.8 us (16%)
  other arithmetic  22.1 us (7%)
  starting transfers between devices  21.3 us (7%)
  waiting for transfers between devices  7.67 us (2%)
    dynamic_update_slice x1692, local copies, waits for them, and re-layouts, coef_factor(): lax.scan(coef_downward, (second_low, second_up), (below[2:], middle[2:],...  83.8 us
    all_gather x2, blocking collectives, along_vel(): lax.all_gather(src_rows, 'vel', axis=0, tiled=True)  23.7 us
    dynamic_slice x1692, local copies, waits for them, and re-layouts, coef_factor(): lax.scan(coef_downward, (second_low, second_up), (below[2:], middle[2:],...  19.4 us
    all_gather x2, blocking collectives, along_pos(): lax.all_gather(src_rows, 'pos', axis=0, tiled=True)  19.3 us
    ppermute x4, starting transfers between devices, extended(): lax.ppermute(tail, axis, [(i, (i + 1) % count) for i in range(ends)])  16.2 us
    another operation x4, loops' own time, eliminate(): lax.scan(eliminate_downward, start, (fwd_factor[1:], below[2:], source[2:]))  14.5 us
    another operation x4, loops' own time, eliminate(): lax.scan(eliminate_upward, jnp.zeros_like(start), (fwd_up[:-1], fwd_src[:...  13.5 us
    all_gather x1, blocking collectives, along_vel(): lax.all_gather(low_rows, 'vel', axis=0, tiled=True)  13 us

commit v1 on v0

v1 whole, which is shorter than its diff:
```python
import functools
import math

import jax
import jax.numpy as jnp
from jax import lax
from jax.experimental import pallas as pl
from jax.experimental.pallas import tpu as pltpu
from jax.sharding import PartitionSpec as P

STEPS = 2
NPHASE = 64
SUB = 8
MESH = pl.DeviceIdType.MESH


def coef_chain(low, high, excess):
    inv, carry_low, ups, lows, rest = [], [], [], [], []
    for t in range(len(low)):
        if t == 0:
            left_low, left_rest = low[0], excess[0]
        else:
            left_low, left_rest = low[t] * lows[-1], low[t] * rest[-1] + excess[t]
        factor = 1.0 / (left_low + left_rest + high[t])
        inv.append(factor)
        carry_low.append(low[t] * factor)
        ups.append(high[t] * factor)
        lows.append(left_low * factor)
        rest.append(left_rest * factor)
    beta, gamma, eps = lows[-1], ups[-1], rest[-1]
    betas, gammas, epss = [beta], [gamma], [eps]
    for t in range(len(low) - 2, -1, -1):
        beta = lows[t] + ups[t] * beta
        gamma = ups[t] * gamma
        eps = rest[t] + ups[t] * eps
        betas.append(beta)
        gammas.append(gamma)
        epss.append(eps)
    return inv, carry_low, ups, betas[::-1], gammas[::-1], epss[::-1]


def source_chain(chain, source):
    inv, carry_low, ups = chain[:3]
    forward = [source[0] * inv[0]]
    for t in range(1, len(source)):
        forward.append(source[t] * inv[t] + carry_low[t] * forward[-1])
    own = [forward[-1]]
    for t in range(len(source) - 2, -1, -1):
        own.append(forward[t] + ups[t] * own[-1])
    return own[::-1]


def next_sub(x, axis):
    return pltpu.roll(x, SUB - 1, axis)


def factor_block(coef, store_row):
    one = jnp.ones_like(coef[0])
    inner = coef_chain(coef[:-1], coef[:-1], [one] * (len(coef) - 1))
    beta, gamma, eps = inner[3:]
    last = coef[-1]
    low = last * beta[-1]
    high = last * next_sub(gamma[0], 0)
    excess = 1.0 + last * eps[-1] + last * next_sub(eps[0], 0)
    rows = lambda x: [x[s : s + 1] for s in range(SUB - 1)]
    outer = coef_chain(rows(low), rows(high), rows(excess))
    obeta, ogamma, oeps = outer[3:]
    end = slice(SUB - 1, SUB)
    first_gamma = gamma[0][0:1]
    store_row(0, beta[0][0:1] + first_gamma * obeta[0])
    store_row(1, first_gamma * ogamma[0])
    store_row(2, eps[0][0:1] + first_gamma * oeps[0])
    store_row(3, last[end])
    store_row(4, low[end] * obeta[-1])
    store_row(5, 1.0 + last[end] * eps[-1][end] + low[end] * oeps[-1])
    return inner, outer, last, first_gamma, low[end]


def eliminate(block, source, hold_a, hold_b):
    inner, outer, last, first_gamma, end_low = block
    planes = source[0].shape[0]
    own = source_chain(inner, source[:-1])
    sub = lax.broadcasted_iota(jnp.int32, source[0].shape, 1)
    after = jnp.where(sub == SUB - 1, 0.0, next_sub(own[0], 1))
    seps = source[-1] + last * (own[-1] + after)
    hold_a[...] = seps.reshape(hold_a.shape)
    hold_b[...] = own[0].reshape(hold_b.shape)
    row = lambda ref, s: ref[pl.ds(s, planes, stride=SUB), :]
    outer_own = source_chain(outer, [row(hold_a, s) for s in range(SUB - 1)])
    first = row(hold_b, 0) + first_gamma * outer_own[0]
    own_end = row(hold_a, SUB - 1) + end_low * outer_own[-1]
    return own, outer_own, first, own_end


def finish(block, own, outer_own, before, end, hold_a, hold_b):
    inner, outer = block[:2]
    planes = before.shape[0]
    hold_b[pl.ds(0, planes, stride=SUB), :] = before
    for s in range(SUB - 1):
        value = outer_own[s] + outer[3][s] * before + outer[4][s] * end
        hold_a[pl.ds(s, planes, stride=SUB), :] = value
        hold_b[pl.ds(s + 1, planes, stride=SUB), :] = value
    hold_a[pl.ds(SUB - 1, planes, stride=SUB), :] = end
    right = hold_a[...].reshape(own[0].shape)
    left = hold_b[...].reshape(own[0].shape)
    return [p + b * left + g * right for p, b, g in zip(own, inner[3], inner[4])] + [right]


def reduced_coefs(buf, count):
    kept, rest = [], 1.0
    for d in range(count):
        link = buf[d, 3:4, :]
        left = buf[d, 4:5, :]
        high = link * buf[d + 1, 1:2, :]
        excess = left * rest + buf[d, 5:6, :] + link * buf[d + 1, 2:3, :]
        factor = 1.0 / (excess + high)
        rest = excess * factor
        kept.append((factor, left * factor, high * factor, link * factor))
    return kept


def reduced_solve(kept, buf, step, whole, count, planes):
    forward, prior = [], None
    for d in range(count):
        factor, left, _, link = kept[d]
        value = factor * buf[step, d, planes : 2 * planes, :] + link * buf[step, d + 1, 0:planes, :]
        prior = value if prior is None else value + left * prior
        forward.append(prior)
    value = forward[-1]
    whole[count] = value
    for d in range(count - 2, -1, -1):
        value = forward[d] + kept[d][2] * value
        whole[d + 1] = value


def kernel(
    npos, nvel, planes, cells, width,
    dens, pcoef, vcoef, mask, phase,
    out, taken,
    ext, turned, edge_tmp, vext, pos_edge, vel_edge, pos_edge_in, vel_edge_in,
    pos_cbuf, vel_cbuf, pos_buf, vel_buf, pos_whole, vel_whole, hold_a, hold_b,
    edge_send, edge_recv, psend, precv, vsend, vrecv,
):
    lanes = width
    mp, mv = cells // SUB, width // SUB
    ipos, ivel = lax.axis_index("pos"), lax.axis_index("vel")

    pos_id = lambda d: (d, ivel)
    vel_id = lambda d: (ipos, d)

    barrier = pltpu.get_barrier_semaphore()

    def greet(count, me, ident):
        for off in range(1, count):
            peer = lax.rem(me + off, count)
            pl.semaphore_signal(barrier, 1, device_id=ident(peer), device_id_type=MESH)

    pos_edge_in[...] = jnp.zeros_like(pos_edge_in)
    vel_edge_in[...] = jnp.zeros_like(vel_edge_in)
    greet(npos, ipos, pos_id)
    greet(nvel, ivel, vel_id)
    ext[...] = jnp.zeros_like(ext)
    vext[...] = jnp.zeros_like(vext)
    edge_tmp[...] = jnp.zeros_like(edge_tmp)
    for cbuf, buf, whole, count in (
        (pos_cbuf, pos_buf, pos_whole, npos),
        (vel_cbuf, vel_buf, vel_whole, nvel),
    ):
        sub = lax.broadcasted_iota(jnp.int32, (8, lanes), 0)
        cbuf[count] = jnp.where(sub == 2, 1.0, 0.0)
        buf[0, count] = jnp.zeros((2 * planes, lanes), jnp.float32)
        buf[1, count] = jnp.zeros((2 * planes, lanes), jnp.float32)
        whole[0] = jnp.zeros((planes, lanes), jnp.float32)
        whole[count + 1] = jnp.zeros((planes, lanes), jnp.float32)

    hit = mask[...].astype(jnp.float32)
    pos_edge[...] = jnp.zeros_like(pos_edge)
    for p in range(planes):
        pos_edge[p : p + 1, :] = dens[p * cells : p * cells + 1, :]
        pos_edge[planes + p : planes + p + 1, :] = dens[(p + 1) * cells - 1 : (p + 1) * cells, :]
    pos_edge[2 * planes : 2 * planes + 1, :] = hit[0:1]
    pos_edge[2 * planes + 1 : 2 * planes + 2, :] = hit[cells - 1 : cells]
    pos_edge[2 * planes + 2 : 2 * planes + 3, :] = vcoef[0:1, :]
    pos_edge[2 * planes + 3 : 2 * planes + 4, :] = vcoef[cells - 1 : cells, :]
    lane = lax.broadcasted_iota(jnp.int32, (cells, lanes), 1)
    gathered = jnp.zeros((cells, lanes), jnp.float32)
    for p in range(planes):
        one = dens[p * cells : (p + 1) * cells, :]
        gathered = jnp.where(lane == p, one[:, 0:1], gathered)
        gathered = jnp.where(lane == planes + p, one[:, lanes - 1 : lanes], gathered)
    gathered = jnp.where(lane == 2 * planes, hit[:, 0:1], gathered)
    gathered = jnp.where(lane == 2 * planes + 1, hit[:, lanes - 1 : lanes], gathered)
    edge_tmp[0:cells, :] = gathered
    vel_edge[...] = edge_tmp[...].T[0:16]

    pl.semaphore_wait(barrier, (npos - 1) + (nvel - 1))

    def edge_copy(axis, to_right, src, dst, ident, me):
        slot = 0 if to_right else 1
        peer = me + 1 if to_right else me - 1
        return pltpu.make_async_remote_copy(
            src_ref=src, dst_ref=dst.at[slot],
            send_sem=edge_send.at[axis, slot], recv_sem=edge_recv.at[axis, slot],
            device_id=ident(peer), device_id_type=MESH,
        )

    sides = (
        (0, pos_edge, pos_edge_in, pos_id, ipos, npos),
        (1, vel_edge, vel_edge_in, vel_id, ivel, nvel),
    )

    def edge_each(which, act):
        axis, src, dst, ident, me, count = sides[which]

        @pl.when(me < count - 1)
        def _():
            act(edge_copy(axis, True, src, dst, ident, me), True)

        @pl.when(me > 0)
        def _():
            act(edge_copy(axis, False, src, dst, ident, me), False)

    def edge_wait(which):
        axis, src, dst, ident, me, count = sides[which]

        @pl.when(me > 0)
        def _():
            edge_copy(axis, True, src, dst, ident, me).wait_recv()

        @pl.when(me < count - 1)
        def _():
            edge_copy(axis, False, src, dst, ident, me).wait_recv()

    edge_each(0, lambda c, _: c.start())
    edge_each(1, lambda c, _: c.start())

    def spread_copy(ref, kind, sends, recvs, ident, me, count, off):
        peer = lax.rem(me + off, count)
        return pltpu.make_async_remote_copy(
            src_ref=ref.at[me], dst_ref=ref.at[me],
            send_sem=sends.at[kind, off], recv_sem=recvs.at[kind, me],
            device_id=ident(peer), device_id_type=MESH,
        )

    def spread(*args):
        for off in range(1, args[-1]):
            spread_copy(*args, off).start()

    def spread_wait_recv(ref, kind, sends, recvs, ident, me, count):
        for off in range(1, count):
            sender = lax.rem(me + off, count)
            pltpu.make_async_remote_copy(
                src_ref=ref.at[sender], dst_ref=ref.at[sender],
                send_sem=sends.at[kind, off], recv_sem=recvs.at[kind, sender],
                device_id=ident(sender), device_id_type=MESH,
            ).wait_recv()

    def spread_wait_send(*args):
        for off in range(1, args[-1]):
            spread_copy(*args, off).wait_send()

    pos_coef_args = (pos_cbuf, 0, psend, precv, pos_id, ipos, npos)
    vel_coef_args = (vel_cbuf, 0, vsend, vrecv, vel_id, ivel, nvel)
    pos_args = [(pos_buf.at[i], 1 + i, psend, precv, pos_id, ipos, npos) for i in range(STEPS)]
    vel_args = [(vel_buf.at[i], 1 + i, vsend, vrecv, vel_id, ivel, nvel) for i in range(STEPS)]

    pos_cbuf[ipos] = jnp.zeros((8, lanes), jnp.float32)

    def pos_row(r, value):
        pos_cbuf[ipos, r : r + 1, :] = value

    pos_block = factor_block([pcoef[pl.ds(t, SUB, stride=mp), :] for t in range(mp)], pos_row)
    spread(*pos_coef_args)

    sub = lax.broadcasted_iota(jnp.int32, (SUB, lanes), 0)
    lane = lax.broadcasted_iota(jnp.int32, (SUB, lanes), 1)
    turns = jnp.zeros((SUB, lanes), jnp.int32)
    for p in range(planes):
        turns = jnp.where(sub == p, phase[p], turns)
    cosine = 0.6 * jnp.cos(2.0 * math.pi * turns.astype(jnp.float32) / NPHASE)
    vpos = (2.0 * (ivel * width + lane).astype(jnp.float32) + 1.0) * (1.0 / (width * nvel)) - 1.0
    move = 0.45 * vpos
    move_up, move_down = jnp.maximum(move, 0.0), jnp.minimum(move, 0.0)
    cosines = jnp.stack([jnp.broadcast_to(cosine[p : p + 1], (SUB, lanes)) for p in range(planes)])

    def drift(step, field, row_before, row_after, columns):
        edge_tmp[0 : 2 * planes, :] = columns
        if step > 0:
            edge_tmp[2 * planes : 16, :] = jnp.zeros((16 - 2 * planes, lanes), jnp.float32)
        turned[0:lanes, :] = edge_tmp[...].T
        wide_sub = lax.broadcasted_iota(jnp.int32, (planes, SUB, lanes), 1)
        wide_lane = lax.broadcasted_iota(jnp.int32, (planes, SUB, lanes), 2)
        before = jnp.where(wide_sub == 0, row_before[:, None, :], pltpu.roll(field[-1], 1, 1))
        after = jnp.where(wide_sub == SUB - 1, row_after[:, None, :], next_sub(field[0], 1))
        kept = []
        for t in range(mp):
            xpos = 1.5 * (
                (2.0 * (ipos * cells + sub * mp + t).astype(jnp.float32) + 1.0)
                * (1.0 / (cells * npos))
                - 1.0
            )
            rate = 0.15 * (((xpos - xpos * xpos * xpos)[None] + cosines) - (0.5 * vpos)[None])
            center = field[t]
            back = field[t - 1] if t else before
            ahead = field[t + 1] if t < mp - 1 else after
            cols = turned[pl.ds(t, SUB, stride=mp), :]
            left = jnp.stack([cols[:, p : p + 1] for p in range(planes)])
            right = jnp.stack([cols[:, planes + p : planes + p + 1] for p in range(planes)])
            back_v = jnp.where(wide_lane == 0, left, pltpu.roll(center, 1, 2))
            ahead_v = jnp.where(wide_lane == lanes - 1, right, pltpu.roll(center, lanes - 1, 2))
            along_x = move_up * (center - back) + move_down * (ahead - center)
            along_v = jnp.maximum(rate, 0.0) * (center - back_v) + jnp.minimum(rate, 0.0) * (
                ahead_v - center
            )
            drifted = center - along_x - along_v
            hit_t = mask[pl.ds(t, SUB, stride=mp), :].astype(jnp.float32)
            took = jnp.sum(drifted, axis=0) * hit_t
            if step > 0:
                took = taken[pl.ds(t, SUB, stride=mp), :] + took
            taken[pl.ds(t, SUB, stride=mp), :] = took
            kept.append(drifted * (1.0 - hit_t))
        return kept

    edge_wait(1)
    edge_wait(0)
    row_before = pos_edge_in[0, planes : 2 * planes, :]
    row_after = pos_edge_in[1, 0:planes, :]
    keep_before = 1.0 - pos_edge_in[0, 2 * planes + 1 : 2 * planes + 2, :]
    keep_after = 1.0 - pos_edge_in[1, 2 * planes : 2 * planes + 1, :]
    col_keep_left = 1.0 - vel_edge_in[0, 2 * planes + 1 : 2 * planes + 2, :]
    col_keep_right = 1.0 - vel_edge_in[1, 2 * planes : 2 * planes + 1, :]
    columns = jnp.concatenate(
        [vel_edge_in[0, planes : 2 * planes, :], vel_edge_in[1, 0:planes, :]], axis=0
    )
    field = [
        jnp.stack([dens[pl.ds(p * cells + t, SUB, stride=mp), :] for p in range(planes)])
        for t in range(mp)
    ]
    vel_block = pos_kept = vel_kept = None

    for step in range(STEPS):
        kept = drift(step, field, row_before, row_after, columns)
        own, outer_own, first, own_end = eliminate(pos_block, kept, hold_a, hold_b)
        pos_buf[step, ipos, 0:planes, :] = first
        pos_buf[step, ipos, planes : 2 * planes, :] = own_end
        spread(*pos_args[step])
        if step == 0:
            vext[0:cells, :] = vcoef[...]
            vext[cells : cells + 1, :] = pos_edge_in[0, 2 * planes + 3 : 2 * planes + 4, :]
            vext[cells + 1 : cells + 2, :] = pos_edge_in[1, 2 * planes + 2 : 2 * planes + 3, :]
            turned[0:width, :] = vext[...].T
            vel_cbuf[ivel] = jnp.zeros((8, lanes), jnp.float32)

            def vel_row(r, value):
                vel_cbuf[ivel, r : r + 1, :] = value

            vel_block = factor_block(
                [turned[pl.ds(t, SUB, stride=mv), :] for t in range(mv)], vel_row
            )
            spread(*vel_coef_args)
            spread_wait_recv(*pos_coef_args)
            pos_kept = reduced_coefs(pos_cbuf, npos)
        spread_wait_recv(*pos_args[step])
        reduced_solve(pos_kept, pos_buf, step, pos_whole, npos, planes)
        before, end, beyond = pos_whole[ipos], pos_whole[ipos + 1], pos_whole[ipos + 2]
        swept = finish(pos_block, own, outer_own, before, end, hold_a, hold_b)
        for t in range(mp):
            for p in range(planes):
                ext[pl.ds(p * lanes + t, SUB, stride=mp), :] = swept[t][p]
        ext[pl.ds(cells, planes, stride=lanes), :] = before
        ext[pl.ds(cells + 1, planes, stride=lanes), :] = (
            pos_buf[step, ipos + 1, 0:planes, :]
            + pos_cbuf[ipos + 1, 0:1, :] * end
            + pos_cbuf[ipos + 1, 1:2, :] * beyond
        )
        for p in range(planes):
            turned[p * width : (p + 1) * width, :] = ext[p * lanes : (p + 1) * lanes, :].T
        source = [
            jnp.stack([turned[pl.ds(p * width + t, SUB, stride=mv), :] for p in range(planes)])
            for t in range(mv)
        ]
        own, outer_own, first, own_end = eliminate(vel_block, source, hold_a, hold_b)
        vel_buf[step, ivel, 0:planes, :] = first
        vel_buf[step, ivel, planes : 2 * planes, :] = own_end
        spread(*vel_args[step])
        if step == 0:
            spread_wait_recv(*vel_coef_args)
            vel_kept = reduced_coefs(vel_cbuf, nvel)
        spread_wait_recv(*vel_args[step])
        reduced_solve(vel_kept, vel_buf, step, vel_whole, nvel, planes)
        before, end, beyond = vel_whole[ivel], vel_whole[ivel + 1], vel_whole[ivel + 2]
        solved = finish(vel_block, own, outer_own, before, end, hold_a, hold_b)
        for t in range(mv):
            for p in range(planes):
                turned[pl.ds(p * width + t, SUB, stride=mv), :] = solved[t][p]
        if step < STEPS - 1:
            for p in range(planes):
                ext[p * lanes : (p + 1) * lanes, :] = turned[p * width : (p + 1) * width, :].T
            field = []
            for t in range(mp):
                keep = 1.0 - mask[pl.ds(t, SUB, stride=mp), :].astype(jnp.float32)
                field.append(
                    jnp.stack(
                        [ext[pl.ds(p * lanes + t, SUB, stride=mp), :] for p in range(planes)]
                    )
                    * keep
                )
            row_before = ext[pl.ds(cells, planes, stride=lanes), :] * keep_before
            row_after = ext[pl.ds(cells + 1, planes, stride=lanes), :] * keep_after
            following = (
                vel_buf[step, ivel + 1, 0:planes, :]
                + vel_cbuf[ivel + 1, 0:1, :] * end
                + vel_cbuf[ivel + 1, 1:2, :] * beyond
            )
            columns = jnp.concatenate([before * col_keep_left, following * col_keep_right], axis=0)
        else:
            keep = 1.0 - mask[...].astype(jnp.float32)
            for p in range(planes):
                result = turned[p * width : (p + 1) * width, :].T
                out[p * cells : (p + 1) * cells, :] = result[0:cells] * keep

    edge_each(0, lambda c, _: c.wait_send())
    edge_each(1, lambda c, _: c.wait_send())
    for args in [pos_coef_args, vel_coef_args] + pos_args + vel_args:
        spread_wait_send(*args)


def on_device(npos, nvel, density, pos_coef, vel_coef, exit_mask, phase_index):
    planes, cells, width = density.shape
    f32 = jnp.float32
    vmem = pl.BlockSpec(memory_space=pltpu.VMEM)
    dma = pltpu.SemaphoreType.DMA
    scratch = lambda *shape: pltpu.VMEM(shape, f32)
    field, absorbed = pl.pallas_call(
        functools.partial(kernel, npos, nvel, planes, cells, width),
        out_shape=(
            jax.ShapeDtypeStruct((planes * cells, width), f32),
            jax.ShapeDtypeStruct((cells, width), f32),
        ),
        in_specs=[vmem] * 4 + [pl.BlockSpec(memory_space=pltpu.SMEM)],
        out_specs=(vmem, vmem),
        scratch_shapes=[
            scratch(planes * 128, width),
            scratch(planes * width, 128),
            scratch(128, width),
            scratch(128, width),
            scratch(16, width),
            scratch(16, width),
            scratch(2, 16, width),
            scratch(2, 16, width),
            scratch(npos + 1, 8, width),
            scratch(nvel + 1, 8, width),
            scratch(STEPS, npos + 1, 2 * planes, width),
            scratch(STEPS, nvel + 1, 2 * planes, width),
            scratch(npos + 2, planes, width),
            scratch(nvel + 2, planes, width),
            scratch(planes * SUB, width),
            scratch(planes * SUB, width),
            dma((2, 2)),
            dma((2, 2)),
            dma((1 + STEPS, npos)),
            dma((1 + STEPS, npos)),
            dma((1 + STEPS, nvel)),
            dma((1 + STEPS, nvel)),
        ],
        compiler_params=pltpu.CompilerParams(
            collective_id=0, has_side_effects=True, vmem_limit_bytes=24 * 1024 * 1024
        ),
        cost_estimate=pl.CostEstimate(
            flops=2_000_000, bytes_accessed=400_000, transcendentals=1024
        ),
        name="line_solves",
    )(density.reshape(planes * cells, width), pos_coef, vel_coef, exit_mask, phase_index)
    return field.reshape(planes, cells, width), absorbed


def solution(mesh):
    return jax.shard_map(
        functools.partial(on_device, mesh.shape["pos"], mesh.shape["vel"]),
        mesh=mesh,
        in_specs=(P(None, "pos", "vel"), P("pos", "vel"), P("pos", "vel"), P("pos", "vel"), P()),
        out_specs=(P(None, "pos", "vel"), P("pos", "vel")),
        check_vma=False,
    )
```

time: 309 us -> 30.4 us (0.10)
  local copies, waits for them, and re-layouts: 119 us -> 5.1 us
  blocking collectives: 85.5 us -> 0 us
  loops' own time: 50.8 us -> 0 us
  Pallas kernels: 0 us -> 24.3 us
  other arithmetic: 22.1 us -> 0 us
  starting transfers between devices: 21.3 us -> 0 us
  waiting for transfers between devices: 7.67 us -> 0 us
    dynamic_update_slice x1836 -> x0, local copies, waits for them, and re-layouts: 91.9 us -> none  [the longest x1692 83.8 us: coef_factor(): lax.scan(coef_downward, (second_low, second_up), (below[2:], middle[2:],...]
    all_gather x8 -> x0, blocking collectives: 85.5 us -> none  [the longest x2 23.7 us: along_vel(): lax.all_gather(src_rows, 'vel', axis=0, tiled=True)]
    another operation x20 -> x0, loops' own time: 50.8 us -> none  [the longest x4 14.5 us: eliminate(): lax.scan(eliminate_downward, start, (fwd_factor[1:], below[2:], source[2:]))]
    pallas_call x0 -> x1, Pallas kernels: none -> 24.3 us  [on_device(): pl.pallas_call(functools.partial(kernel, npos, nvel, planes, cells, width...]
    ppermute x8 -> x0, starting transfers between devices: 21.3 us -> none  [the longest x4 16.2 us: extended(): lax.ppermute(tail, axis, [(i, (i + 1) % count) for i in range(ends)])]
    dynamic_slice x1836 -> x0, local copies, waits for them, and re-layouts: 21 us -> none  [the longest x1692 19.4 us: coef_factor(): lax.scan(coef_downward, (second_low, second_up), (below[2:], middle[2:],...]
    mul x1006 -> x0, other arithmetic: 14.2 us -> none  [the longest x376 4.95 us: coef_downward(): result = (-factor * row_low * prior_low, factor * row_up)]
    ppermute x8 -> x0, waiting for transfers between devices: 7.67 us -> none  [the longest x4 4.02 us: extended(): lax.ppermute(head, axis, [((i + 1) % count, i) for i in range(ends)])]
where the time goes in v1:
time: 30.4 us; the launch traced here: 30 us
  Pallas kernels  24.3 us (80%)
  local copies, waits for them, and re-layouts  5.1 us (17%)
  between operations  0.65 us (2%)
    pallas_call x1, Pallas kernels, on_device(): pl.pallas_call(functools.partial(kernel, npos, nvel, planes, cells, width...  24.3 us
    unnamed x12, local copies, waits for them, and re-layouts  5.1 us

profile of v1, /device:TPU:0, one launch (start us, length us, event | category | flops | bytes accessed | tf_op | source)
XLA Modules:
  0.0 30.0 jit_solution(2369175546555052094)
XLA Ops:
  0.6 0.0 copy-start.4
  0.6 0.6 %copy-done.4 = s32[4]{0:T(128)S(1)} copy-done((s32[4]{0:T(128)S(1)}, s32[4]{0:T(128)}, u32[]{:S(2)}) %copy-start.4) | copy-done | bytes 40
  1.3 0.0 copy-start
  1.3 0.9 %copy-done = f32[4,64,128]{2,1,0:T(8,128)S(1)} copy-done((f32[4,64,128]{2,1,0:T(8,128)S(1)}, f32[4,64,128]{2,1,0:T(8,128)}, u32[]{:S(2)}) %copy-start) | copy-done | bytes 131096
  2.2 0.0 copy-start.1
  2.2 0.8 %copy-done.1 = f32[64,128]{1,0:T(8,128)S(1)} copy-done((f32[64,128]{1,0:T(8,128)S(1)}, f32[64,128]{1,0:T(8,128)}, u32[]{:S(2)}) %copy-start.1) | copy-done | bytes 32792
  3.0 0.0 copy-start.2
  3.0 0.8 %copy-done.2 = f32[64,128]{1,0:T(8,128)S(1)} copy-done((f32[64,128]{1,0:T(8,128)S(1)}, f32[64,128]{1,0:T(8,128)}, u32[]{:S(2)}) %copy-start.2) | copy-done | bytes 32792
  3.7 0.0 copy-start.3
  3.7 0.8 %copy-done.3 = s32[64,128]{1,0:T(8,128)S(1)} copy-done((s32[64,128]{1,0:T(8,128)S(1)}, s32[64,128]{1,0:T(8,128)}, u32[]{:S(2)}) %copy-start.3) | copy-done | bytes 32792
  4.5 24.3 %line_solves.1 = (f32[256,128]{1,0:T(8,128)S(1)}, f32[64,128]{1,0:T(8,128)S(1)}) custom-call(f32[256,128]{1,0:T(8,128)S(1)} %bitcast.2, f32[64,128]{1,0:T(8,128)S(1)} %copy-done.1, f32[64,128]{1,0:T(8,128)S(1)} %copy-done.2, s32[64,128]{1,0:T(8,128)S(1)} %copy-done.3, s32[4]{0:T(128)S(1)} %copy-done.4), custom_call_target="tpu_custom_call" | custom-call | flops 2000000 | bytes 400000 | tf_op jit(solution)/shard_map/line_solves/pallas_call | solution.py:434
  28.8 0.7 %copy.9 = f32[4,64,128]{2,1,0:T(8,128)} copy(f32[4,64,128]{2,1,0:T(8,128)S(1)} %bitcast.3) | data formatting | bytes 262144
  29.4 0.6 %copy.10 = f32[64,128]{1,0:T(8,128)} copy(f32[64,128]{1,0:T(8,128)S(1)} %get-tuple-element.9) | data formatting | bytes 65536
Async XLA Ops:
  0.6 0.7 %copy-start.4 = (s32[4]{0:T(128)S(1)}, s32[4]{0:T(128)}, u32[]{:S(2)}) copy-start(s32[4]{0:T(128)} %phase.1) | copy-start | bytes 52
  1.3 0.9 %copy-start = (f32[4,64,128]{2,1,0:T(8,128)S(1)}, f32[4,64,128]{2,1,0:T(8,128)}, u32[]{:S(2)}) copy-start(f32[4,64,128]{2,1,0:T(8,128)} %param.5) | copy-start | bytes 393220
  2.2 0.8 %copy-start.1 = (f32[64,128]{1,0:T(8,128)S(1)}, f32[64,128]{1,0:T(8,128)}, u32[]{:S(2)}) copy-start(f32[64,128]{1,0:T(8,128)} %pcoef.1) | copy-start | bytes 98308
  3.0 0.8 %copy-start.2 = (f32[64,128]{1,0:T(8,128)S(1)}, f32[64,128]{1,0:T(8,128)}, u32[]{:S(2)}) copy-start(f32[64,128]{1,0:T(8,128)} %vcoef.1) | copy-start | bytes 98308
  3.7 0.8 %copy-start.3 = (s32[64,128]{1,0:T(8,128)S(1)}, s32[64,128]{1,0:T(8,128)}, u32[]{:S(2)}) copy-start(s32[64,128]{1,0:T(8,128)} %mask.1) | copy-start | bytes 98308

commit v2 on v1

--- a/solution.py
+++ b/solution.py
@@ -135,11 +135,12 @@
 
 def kernel(
     npos, nvel, planes, cells, width,
-    dens, pcoef, vcoef, mask, phase,
+    dens_in, pcoef_in, vcoef_in, mask_in, phase_in,
     out, taken,
+    dens, pcoef, vcoef, mask, phase, rates_up, rates_down,
     ext, turned, edge_tmp, vext, pos_edge, vel_edge, pos_edge_in, vel_edge_in,
     pos_cbuf, vel_cbuf, pos_buf, vel_buf, pos_whole, vel_whole, hold_a, hold_b,
-    edge_send, edge_recv, psend, precv, vsend, vrecv,
+    load_sem, edge_send, edge_recv, psend, precv, vsend, vrecv,
 ):
     lanes = width
     mp, mv = cells // SUB, width // SUB
@@ -155,10 +156,24 @@
             peer = lax.rem(me + off, count)
             pl.semaphore_signal(barrier, 1, device_id=ident(peer), device_id_type=MESH)
 
+    loads = [
+        pltpu.make_async_copy(src, dst, load_sem.at[i])
+        for i, (src, dst) in enumerate(
+            (
+                (dens_in, dens),
+                (mask_in, mask),
+                (vcoef_in, vcoef),
+                (pcoef_in, pcoef),
+                (phase_in, phase),
+            )
+        )
+    ]
     pos_edge_in[...] = jnp.zeros_like(pos_edge_in)
     vel_edge_in[...] = jnp.zeros_like(vel_edge_in)
     greet(npos, ipos, pos_id)
     greet(nvel, ivel, vel_id)
+    for load in loads:
+        load.start()
     ext[...] = jnp.zeros_like(ext)
     vext[...] = jnp.zeros_like(vext)
     edge_tmp[...] = jnp.zeros_like(edge_tmp)
@@ -172,6 +187,9 @@
         buf[1, count] = jnp.zeros((2 * planes, lanes), jnp.float32)
         whole[0] = jnp.zeros((planes, lanes), jnp.float32)
         whole[count + 1] = jnp.zeros((planes, lanes), jnp.float32)
+
+    for load in loads:
+        load.wait()
 
     hit = mask[...].astype(jnp.float32)
     pos_edge[...] = jnp.zeros_like(pos_edge)
@@ -193,8 +211,6 @@
     edge_tmp[0:cells, :] = gathered
     vel_edge[...] = edge_tmp[...].T[0:16]
 
-    pl.semaphore_wait(barrier, (npos - 1) + (nvel - 1))
-
     def edge_copy(axis, to_right, src, dst, ident, me):
         slot = 0 if to_right else 1
         peer = me + 1 if to_right else me - 1
@@ -231,9 +247,6 @@
         def _():
             edge_copy(axis, False, src, dst, ident, me).wait_recv()
 
-    edge_each(0, lambda c, _: c.start())
-    edge_each(1, lambda c, _: c.start())
-
     def spread_copy(ref, kind, sends, recvs, ident, me, count, off):
         peer = lax.rem(me + off, count)
         return pltpu.make_async_remote_copy(
@@ -270,8 +283,6 @@
         pos_cbuf[ipos, r : r + 1, :] = value
 
     pos_block = factor_block([pcoef[pl.ds(t, SUB, stride=mp), :] for t in range(mp)], pos_row)
-    spread(*pos_coef_args)
-
     sub = lax.broadcasted_iota(jnp.int32, (SUB, lanes), 0)
     lane = lax.broadcasted_iota(jnp.int32, (SUB, lanes), 1)
     turns = jnp.zeros((SUB, lanes), jnp.int32)
@@ -282,6 +293,21 @@
     move = 0.45 * vpos
     move_up, move_down = jnp.maximum(move, 0.0), jnp.minimum(move, 0.0)
     cosines = jnp.stack([jnp.broadcast_to(cosine[p : p + 1], (SUB, lanes)) for p in range(planes)])
+
+    for t in range(mp):
+        xpos = 1.5 * (
+            (2.0 * (ipos * cells + sub * mp + t).astype(jnp.float32) + 1.0) * (1.0 / (cells * npos))
+            - 1.0
+        )
+        rate = 0.15 * (((xpos - xpos * xpos * xpos)[None] + cosines) - (0.5 * vpos)[None])
+        rates_up[t] = jnp.maximum(rate, 0.0)
+        rates_down[t] = jnp.minimum(rate, 0.0)
+
+    pl.semaphore_wait(barrier, (npos - 1) + (nvel - 1))
+
+    edge_each(0, lambda c, _: c.start())
+    edge_each(1, lambda c, _: c.start())
+    spread(*pos_coef_args)
 
     def drift(step, field, row_before, row_after, columns):
         edge_tmp[0 : 2 * planes, :] = columns
@@ -294,12 +320,6 @@
         after = jnp.where(wide_sub == SUB - 1, row_after[:, None, :], next_sub(field[0], 1))
         kept = []
         for t in range(mp):
-            xpos = 1.5 * (
-                (2.0 * (ipos * cells + sub * mp + t).astype(jnp.float32) + 1.0)
-                * (1.0 / (cells * npos))
-                - 1.0
-            )
-            rate = 0.15 * (((xpos - xpos * xpos * xpos)[None] + cosines) - (0.5 * vpos)[None])
             center = field[t]
             back = field[t - 1] if t else before
             ahead = field[t + 1] if t < mp - 1 else after
@@ -309,9 +329,7 @@
             back_v = jnp.where(wide_lane == 0, left, pltpu.roll(center, 1, 2))
             ahead_v = jnp.where(wide_lane == lanes - 1, right, pltpu.roll(center, lanes - 1, 2))
             along_x = move_up * (center - back) + move_down * (ahead - center)
-            along_v = jnp.maximum(rate, 0.0) * (center - back_v) + jnp.minimum(rate, 0.0) * (
-                ahead_v - center
-            )
+            along_v = rates_up[t] * (center - back_v) + rates_down[t] * (ahead_v - center)
             drifted = center - along_x - along_v
             hit_t = mask[pl.ds(t, SUB, stride=mp), :].astype(jnp.float32)
             took = jnp.sum(drifted, axis=0) * hit_t
@@ -434,12 +452,19 @@
     field, absorbed = pl.pallas_call(
         functools.partial(kernel, npos, nvel, planes, cells, width),
         out_shape=(
-            jax.ShapeDtypeStruct((planes * cells, width), f32),
-            jax.ShapeDtypeStruct((cells, width), f32),
+            pltpu.VMEM((planes * cells, width), f32),
+            pltpu.VMEM((cells, width), f32),
         ),
-        in_specs=[vmem] * 4 + [pl.BlockSpec(memory_space=pltpu.SMEM)],
+        in_specs=[pl.BlockSpec(memory_space=pltpu.HBM)] * 5,
         out_specs=(vmem, vmem),
         scratch_shapes=[
+            scratch(planes * cells, width),
+            scratch(cells, width),
+            scratch(cells, width),
+            pltpu.VMEM((cells, width), jnp.int32),
+            pltpu.SMEM((planes,), jnp.int32),
+            scratch(cells // SUB, planes, SUB, width),
+            scratch(cells // SUB, planes, SUB, width),
             scratch(planes * 128, width),
             scratch(planes * width, 128),
             scratch(128, width),
@@ -456,6 +481,7 @@
             scratch(nvel + 2, planes, width),
             scratch(planes * SUB, width),
             scratch(planes * SUB, width),
+            dma((5,)),
             dma((2, 2)),
             dma((2, 2)),
             dma((1 + STEPS, npos)),
@@ -464,7 +490,7 @@
             dma((1 + STEPS, nvel)),
         ],
         compiler_params=pltpu.CompilerParams(
-            collective_id=0, has_side_effects=True, vmem_limit_bytes=24 * 1024 * 1024
+            collective_id=0, has_side_effects=True
         ),
         cost_estimate=pl.CostEstimate(
             flops=2_000_000, bytes_accessed=400_000, transcendentals=1024

time: 30.4 us -> 25.9 us (0.85)
  local copies, waits for them, and re-layouts: 5.1 us -> 1.27 us
  Pallas kernels: 24.3 us -> 23.8 us
    unnamed x12 -> x2, local copies, waits for them, and re-layouts: 5.1 us -> 1.27 us
    pallas_call x1, Pallas kernels: 24.3 us -> 23.8 us  [on_device(): pl.pallas_call(functools.partial(kernel, npos, nvel, planes, cells, width...]
where the time goes in v2:
time: 25.9 us; the launch traced here: 25.7 us
  Pallas kernels  23.8 us (92%)
  local copies, waits for them, and re-layouts  1.27 us (5%)
  between operations  0.64 us (2%)
    pallas_call x1, Pallas kernels, on_device(): pl.pallas_call(functools.partial(kernel, npos, nvel, planes, cells, width...  23.8 us
    unnamed x2, local copies, waits for them, and re-layouts  1.27 us

profile of v2, /device:TPU:0, one launch (start us, length us, event | category | flops | bytes accessed | tf_op | source)
XLA Modules:
  0.0 25.7 jit_solution(12207296978261503011)
XLA Ops:
  0.6 23.8 %line_solves.1 = (f32[256,128]{1,0:T(8,128)S(1)}, f32[64,128]{1,0:T(8,128)S(1)}) custom-call(f32[256,128]{1,0:T(8,128)} %bitcast.3, f32[64,128]{1,0:T(8,128)} %pcoef_in.1, f32[64,128]{1,0:T(8,128)} %vcoef_in.1, s32[64,128]{1,0:T(8,128)} %mask_in.1, s32[4]{0:T(128)} %phase_in.1), custom_call_target="tpu_custom_call" | custom-call | flops 2000000 | bytes 400000 | tf_op jit(solution)/shard_map/line_solves/pallas_call | solution.py:452
  24.4 0.7 %copy.9 = f32[4,64,128]{2,1,0:T(8,128)} copy(f32[4,64,128]{2,1,0:T(8,128)S(1)} %bitcast.2) | data formatting | bytes 262144
  25.1 0.6 %copy.10 = f32[64,128]{1,0:T(8,128)} copy(f32[64,128]{1,0:T(8,128)S(1)} %get-tuple-element.7) | data formatting | bytes 65536

commit v3 on v2

--- a/solution.py
+++ b/solution.py
@@ -188,7 +188,7 @@
         whole[0] = jnp.zeros((planes, lanes), jnp.float32)
         whole[count + 1] = jnp.zeros((planes, lanes), jnp.float32)
 
-    for load in loads:
+    for load in loads[:3]:
         load.wait()
 
     hit = mask[...].astype(jnp.float32)
@@ -277,12 +277,20 @@
     pos_args = [(pos_buf.at[i], 1 + i, psend, precv, pos_id, ipos, npos) for i in range(STEPS)]
     vel_args = [(vel_buf.at[i], 1 + i, vsend, vrecv, vel_id, ivel, nvel) for i in range(STEPS)]
 
+    pl.semaphore_wait(barrier, (npos - 1) + (nvel - 1))
+    edge_each(0, lambda c, _: c.start())
+    edge_each(1, lambda c, _: c.start())
+
+    for load in loads[3:]:
+        load.wait()
     pos_cbuf[ipos] = jnp.zeros((8, lanes), jnp.float32)
 
     def pos_row(r, value):
         pos_cbuf[ipos, r : r + 1, :] = value
 
     pos_block = factor_block([pcoef[pl.ds(t, SUB, stride=mp), :] for t in range(mp)], pos_row)
+    spread(*pos_coef_args)
+
     sub = lax.broadcasted_iota(jnp.int32, (SUB, lanes), 0)
     lane = lax.broadcasted_iota(jnp.int32, (SUB, lanes), 1)
     turns = jnp.zeros((SUB, lanes), jnp.int32)
@@ -302,12 +310,6 @@
         rate = 0.15 * (((xpos - xpos * xpos * xpos)[None] + cosines) - (0.5 * vpos)[None])
         rates_up[t] = jnp.maximum(rate, 0.0)
         rates_down[t] = jnp.minimum(rate, 0.0)
-
-    pl.semaphore_wait(barrier, (npos - 1) + (nvel - 1))
-
-    edge_each(0, lambda c, _: c.start())
-    edge_each(1, lambda c, _: c.start())
-    spread(*pos_coef_args)
 
     def drift(step, field, row_before, row_after, columns):
         edge_tmp[0 : 2 * planes, :] = columns
@@ -376,8 +378,13 @@
                 [turned[pl.ds(t, SUB, stride=mv), :] for t in range(mv)], vel_row
             )
             spread(*vel_coef_args)
+            edge_each(0, lambda c, _: c.wait_send())
+            edge_each(1, lambda c, _: c.wait_send())
+            spread_wait_send(*pos_coef_args)
             spread_wait_recv(*pos_coef_args)
             pos_kept = reduced_coefs(pos_cbuf, npos)
+        if step > 0:
+            spread_wait_send(*vel_args[step - 1])
         spread_wait_recv(*pos_args[step])
         reduced_solve(pos_kept, pos_buf, step, pos_whole, npos, planes)
         before, end, beyond = pos_whole[ipos], pos_whole[ipos + 1], pos_whole[ipos + 2]
@@ -401,7 +408,9 @@
         vel_buf[step, ivel, 0:planes, :] = first
         vel_buf[step, ivel, planes : 2 * planes, :] = own_end
         spread(*vel_args[step])
+        spread_wait_send(*pos_args[step])
         if step == 0:
+            spread_wait_send(*vel_coef_args)
             spread_wait_recv(*vel_coef_args)
             vel_kept = reduced_coefs(vel_cbuf, nvel)
         spread_wait_recv(*vel_args[step])
@@ -437,10 +446,7 @@
                 result = turned[p * width : (p + 1) * width, :].T
                 out[p * cells : (p + 1) * cells, :] = result[0:cells] * keep
 
-    edge_each(0, lambda c, _: c.wait_send())
-    edge_each(1, lambda c, _: c.wait_send())
-    for args in [pos_coef_args, vel_coef_args] + pos_args + vel_args:
-        spread_wait_send(*args)
+    spread_wait_send(*vel_args[-1])
 
 
 def on_device(npos, nvel, density, pos_coef, vel_coef, exit_mask, phase_index):

time: 25.9 us -> 25.8 us (level)
  no operation moved by 1% of the time
where the time goes in v3:
time: 25.8 us; the launch traced here: 25.7 us
  Pallas kernels  23.8 us (92%)
  local copies, waits for them, and re-layouts  1.27 us (5%)
  between operations  0.64 us (2%)
    pallas_call x1, Pallas kernels, on_device(): pl.pallas_call(functools.partial(kernel, npos, nvel, planes, cells, width...  23.8 us
    unnamed x2, local copies, waits for them, and re-layouts  1.27 us

profile of v3, /device:TPU:0, one launch (start us, length us, event | category | flops | bytes accessed | tf_op | source)
XLA Modules:
  0.0 25.7 jit_solution(17055159311917718260)
XLA Ops:
  0.6 23.8 %line_solves.1 = (f32[256,128]{1,0:T(8,128)S(1)}, f32[64,128]{1,0:T(8,128)S(1)}) custom-call(f32[256,128]{1,0:T(8,128)} %bitcast.3, f32[64,128]{1,0:T(8,128)} %pcoef_in.1, f32[64,128]{1,0:T(8,128)} %vcoef_in.1, s32[64,128]{1,0:T(8,128)} %mask_in.1, s32[4]{0:T(128)} %phase_in.1), custom_call_target="tpu_custom_call" | custom-call | flops 2000000 | bytes 400000 | tf_op jit(solution)/shard_map/line_solves/pallas_call | solution.py:458
  24.4 0.7 %copy.9 = f32[4,64,128]{2,1,0:T(8,128)} copy(f32[4,64,128]{2,1,0:T(8,128)S(1)} %bitcast.2) | data formatting | bytes 262144
  25.1 0.6 %copy.10 = f32[64,128]{1,0:T(8,128)} copy(f32[64,128]{1,0:T(8,128)S(1)} %get-tuple-element.7) | data formatting | bytes 65536

commit v4 on v3

--- a/solution.py
+++ b/solution.py
@@ -392,12 +392,13 @@
         for t in range(mp):
             for p in range(planes):
                 ext[pl.ds(p * lanes + t, SUB, stride=mp), :] = swept[t][p]
-        ext[pl.ds(cells, planes, stride=lanes), :] = before
-        ext[pl.ds(cells + 1, planes, stride=lanes), :] = (
-            pos_buf[step, ipos + 1, 0:planes, :]
-            + pos_cbuf[ipos + 1, 0:1, :] * end
-            + pos_cbuf[ipos + 1, 1:2, :] * beyond
-        )
+        if step < STEPS - 1:
+            ext[pl.ds(cells, planes, stride=lanes), :] = before
+            ext[pl.ds(cells + 1, planes, stride=lanes), :] = (
+                pos_buf[step, ipos + 1, 0:planes, :]
+                + pos_cbuf[ipos + 1, 0:1, :] * end
+                + pos_cbuf[ipos + 1, 1:2, :] * beyond
+            )
         for p in range(planes):
             turned[p * width : (p + 1) * width, :] = ext[p * lanes : (p + 1) * lanes, :].T
         source = [

time: 25.8 us -> 25.8 us (level)
  no operation moved by 1% of the time
where the time goes in v4:
time: 25.8 us; the launch traced here: 25.7 us
  Pallas kernels  23.8 us (92%)
  local copies, waits for them, and re-layouts  1.27 us (5%)
  between operations  0.64 us (2%)
    pallas_call x1, Pallas kernels, on_device(): pl.pallas_call(functools.partial(kernel, npos, nvel, planes, cells, width...  23.8 us
    unnamed x2, local copies, waits for them, and re-layouts  1.27 us

profile of v4, /device:TPU:0, one launch (start us, length us, event | category | flops | bytes accessed | tf_op | source)
XLA Modules:
  0.0 25.7 jit_solution(4657039620234792701)
XLA Ops:
  0.6 23.8 %line_solves.1 = (f32[256,128]{1,0:T(8,128)S(1)}, f32[64,128]{1,0:T(8,128)S(1)}) custom-call(f32[256,128]{1,0:T(8,128)} %bitcast.3, f32[64,128]{1,0:T(8,128)} %pcoef_in.1, f32[64,128]{1,0:T(8,128)} %vcoef_in.1, s32[64,128]{1,0:T(8,128)} %mask_in.1, s32[4]{0:T(128)} %phase_in.1), custom_call_target="tpu_custom_call" | custom-call | flops 2000000 | bytes 400000 | tf_op jit(solution)/shard_map/line_solves/pallas_call | solution.py:459
  24.4 0.7 %copy.9 = f32[4,64,128]{2,1,0:T(8,128)} copy(f32[4,64,128]{2,1,0:T(8,128)S(1)} %bitcast.2) | data formatting | bytes 262144
  25.1 0.6 %copy.10 = f32[64,128]{1,0:T(8,128)} copy(f32[64,128]{1,0:T(8,128)S(1)} %get-tuple-element.7) | data formatting | bytes 65536
